TPU v7x, 32 devices: a whole 2x2x4 slice. The times are simulated.
32 devices in a mesh: region: 4 (over z), cell: 8 (over y, x, core).
Axes of the slice: x: 2, y: 2, z: 4, core: 2. Of those that a mesh axis runs over, the one named last changes fastest.
Arguments:
- positions: float32 [3, 128, 512], P(None, ('region', 'cell')), may hold values from 0 to 1
- velocities: float32 [3, 128, 512], P(None, ('region', 'cell')), may hold values from -6 to 6
- mass: float32 [128, 512], P(('region', 'cell')), may hold values from 0.0002 to 0.001
- smoothing: float32 [128, 512], P(('region', 'cell')), may hold values from 0.25 to 0.5
- energy: float32 [128, 512], P(('region', 'cell')), may hold values from 0.5 to 2
- counts: int32 [128], P(('region', 'cell')), may hold values from 128 to 512
- send_cells: int32 [4, 8, 8, 1], P('region', 'cell'), may hold values from -1 to 3, as said below
- local_pairs: int32 [4, 8, 4, 2], P('region', 'cell'), may hold values from 0 to 3, as said below
- edge_cells: int32 [4, 8, 2], P('region', 'cell'), may hold values from 0 to 3
Outputs:
- density: float32 [128, 512], P(('region', 'cell'))
- accel: float32 [3, 128, 512], P(None, ('region', 'cell'))
- energy_rate: float32 [128, 512], P(('region', 'cell'))
Inputs may be any that keep to these rules, and one draw needn't show every extreme that they name: send_cells[r, c, c2, s] is a local cell index of device (r, c), or -1 for an empty slot; slot s is empty from c to c2 exactly when it is empty from c2 to c, and always empty for c2 = c. `local_pairs`: each row holds two different local cell indices of the device.
All inputs are finite; a program needn't handle non-finite values.
Results may differ from a plain program's by a relative error of at most 0.0003.
Values sent between devices are 32-bit elements; how exact they have to be, the bound alone decides.
No kernel may reach another device: no remote copies, remote signals or barrier semaphores. Data moves between devices by JAX's collectives and lax.ppermute only.
A program may use at most 64 MiB of HBM per device.

v0:
```python
import functools
import math

import jax
import jax.numpy as jnp
from jax import lax
from jax.experimental import pallas as pl
from jax.experimental.pallas import tpu as pltpu
from jax.sharding import PartitionSpec as P

GAMMA = 5.0 / 3.0
LANES = 128
BF16 = jnp.bfloat16
F32 = jnp.float32

ROWS = 8
TINY = 1e-12
DOT_K = 48
COLS = 64
STRIP = 16
SENT = 4
SENT_LATER = 5

VMEM = pl.BlockSpec(memory_space=pltpu.VMEM)
SMEM = pl.BlockSpec(memory_space=pltpu.SMEM)
HBM = pl.BlockSpec(memory_space=pltpu.HBM)


def row_ids(shape):
    return lax.broadcasted_iota(jnp.int32, shape, 0)


def split3(value):
    first = value.astype(BF16).astype(F32)
    rest = value - first
    second = rest.astype(BF16).astype(F32)
    return first, second, rest - second


def left_parts(value):
    a, b, c = split3(value)
    return jnp.concatenate([a, a, b, b, a, c], axis=0)


def right_parts(value):
    a, b, c = split3(value)
    return jnp.concatenate([a, b, a, b, c, a], axis=0).astype(BF16)


def norm_row(rows):
    return rows[0:1] * rows[0:1] + rows[1:2] * rows[1:2] + rows[2:3] * rows[2:3]


def left_comps(rows):
    ids = row_ids(rows.shape)
    return jnp.where(ids < 3, rows, jnp.where(ids == 3, norm_row(rows), jnp.where(ids == 4, 1.0, 0.0)))


def right_comps(rows):
    ids = row_ids(rows.shape)
    return jnp.where(ids < 3, -2.0 * rows, jnp.where(ids == 3, 1.0, jnp.where(ids == 4, norm_row(rows), 0.0)))


def chunks(count, size):
    return lax.shift_right_logical(count + (size - 1), jnp.int32(size.bit_length() - 1))


class Meta:
    def __init__(self, cells, peers, pairs):
        self.cells, self.peers, self.pairs = cells, peers, pairs
        self.send = cells
        self.pair = cells + peers
        self.edge = self.pair + 2 * pairs
        self.size = self.edge + 2


def prep_kernel(
    lay,
    counts_in, send_in, pairs_in, edge_in, pos_in, vel_in, mass_in, smooth_in,
    own, pay, odd, meta,
    counts, send, pairs, edge, pos, vel, mass, smooth, sems,
):
    inputs = (counts_in, send_in, pairs_in, edge_in, pos_in, vel_in, mass_in, smooth_in)
    buffers = (counts, send, pairs, edge, pos, vel, mass, smooth)
    copies = [
        pltpu.make_async_copy(source, target, sems.at[k])
        for k, (source, target) in enumerate(zip(inputs, buffers))
    ]
    for copy in copies:
        copy.start()
    for copy in copies:
        copy.wait()
    cells = mass.shape[0]
    slots = mass.shape[1]
    for k in range(cells):
        meta[k] = counts[k]
    for k in range(lay.peers):
        meta[lay.send + k] = send[k]
    for k in range(lay.pairs):
        for side in range(2):
            meta[lay.pair + 2 * k + side] = pairs[0, 0, side, k]
    for side in range(2):
        meta[lay.edge + side] = edge[0, 0, side]

    lane = lax.broadcasted_iota(jnp.int32, (1, slots), 1)
    for k in range(cells):
        live = lane < counts[k]
        for d in range(3):
            own[k, d : d + 1, :] = pos[d, k : k + 1, :] - 0.5
            own[k, 5 + d : 6 + d, :] = vel[d, k : k + 1, :]
        own[k, 3:4, :] = jnp.where(live, mass[k : k + 1, :], 0.0)
        own[k, 4:5, :] = smooth[k : k + 1, :]

    def row(cell, r):
        return own[cell, r : r + 1, :]

    fill(lay, pay, odd, meta, SENT, row)


def fill(lay, pay, odd, meta, count, row):
    slots = pay.shape[2] // count
    side = lax.axis_index("side")
    first = side * lay.peers
    pay[...] = jnp.zeros_like(pay)

    def put(out, at, cell, keep):
        for r in range(count):
            value = row(cell, r)
            if keep is not None:
                value = jnp.where(keep, value, 0.0)
            out[at, :, r * slots : (r + 1) * slots] = value

    def peer(k, carry):
        picked = meta[lay.send + k]
        put(pay, first + k, jnp.maximum(picked, 0), picked >= 0)
        return carry

    lax.fori_loop(0, lay.peers, peer, 0)
    put(pay, lay.peers - first + lax.axis_index("cell"), meta[lay.edge + 1 - side], None)
    put(odd, 0, meta[lay.edge + side], None)


def arrivals(lay):
    first = lax.axis_index("side") * lay.peers
    return first, lay.peers - first + lax.axis_index("cell")


class Tiles:
    FIELDS = 7

    def __init__(self, icut, jcut, table):
        self.icut, self.jcut, self.table = icut, jcut, table
        self.count = self.blocks = jnp.int32(0)

    def push(self, a, b, w, ok, i, ni, j, nj):
        at = self.FIELDS * self.count
        for field, value in enumerate((a, b, w, i, ni, j, nj)):
            self.table[at + field] = value
        self.count = self.count + ok.astype(jnp.int32)
        self.blocks = self.blocks + jnp.where(ok, ni * nj, 0)

    def whole(self, a, b, w, ok, alive, blive):
        self.push(a, b, w, ok, 0, chunks(alive, self.icut), 0, chunks(blive, self.jcut))

    def close(self):
        self.push(0, 0, 0, jnp.bool_(False), 0, 1, 0, 1)


def local_tiles(tiles, lay, meta, both):
    cells = lay.cells
    one = jnp.int32(1)

    def key(row):
        first = meta[lay.pair + 2 * row]
        second = meta[lay.pair + 2 * row + 1]
        return jnp.minimum(first, second) * cells + jnp.maximum(first, second)

    keys = [key(row) for row in range(lay.pairs)]
    for a in range(cells):
        for b in range(a + 1, cells):
            mult = jnp.int32(0)
            for pair in keys:
                mult = mult + (pair == a * cells + b).astype(jnp.int32)
            tiles.whole(a, b, mult, mult > 0, meta[a], meta[b])
            if not both:
                tiles.whole(b, a, mult, mult > 0, meta[b], meta[a])
    if not both:
        for a in range(cells):
            tiles.whole(a, a, one, meta[a] > 0, meta[a], meta[a])
        tiles.close()
        return None
    span = tiles.jcut // tiles.icut
    for a in range(cells):
        tiles.push(a, a, one, meta[a] > tiles.jcut, 0, span, 1, chunks(meta[a], tiles.jcut) - 1)
    mutual = tiles.blocks
    for a in range(cells):
        rows = chunks(meta[a], tiles.icut)
        tiles.push(a, a, one, meta[a] > 0, 0, jnp.minimum(rows, span), 0, 1)
        tiles.push(a, a, one, meta[a] > tiles.jcut, span, rows - span, 1, 1)
    tiles.close()
    return mutual


def remote_tiles(tiles, lay, meta, live):
    one = jnp.int32(1)
    for k in range(lay.peers):
        picked = meta[lay.send + k]
        a = jnp.maximum(picked, 0)
        tiles.whole(a, k, one, (picked >= 0) & (live[k] > 0), meta[a], live[k])
    side = lax.axis_index("side")
    for b, edge in ((lay.peers, 1 - side), (lay.peers + 1, side)):
        a = meta[lay.edge + edge]
        tiles.whole(a, b, one, live[b] > 0, meta[a], live[b])
    tiles.close()


class Blocks:
    FIELDS = 5

    def __init__(self, tiles, ring):
        self.icut, self.jcut = tiles.icut, tiles.jcut
        self.table, self.last = tiles.table, tiles.count
        self.ring, self.total = ring, tiles.blocks

    def clear(self, entries):
        for k in range(entries * self.FIELDS):
            self.ring[k] = 0

    def write(self, slot, state):
        n, ii, jj = state
        a, b, w, i, ni, j, nj = (self.table[Tiles.FIELDS * n + k] for k in range(Tiles.FIELDS))
        for field, value in enumerate((a, b, (i + ii) * self.icut, (j + jj) * self.jcut, w)):
            self.ring[self.FIELDS * slot + field] = value
        jwrap = jj + 1 >= nj
        inext = jnp.where(jwrap, ii + 1, ii)
        iwrap = inext >= ni
        return (
            jnp.minimum(jnp.where(iwrap, n + 1, n), self.last),
            jnp.where(iwrap, 0, inext),
            jnp.where(jwrap, 0, jj + 1),
        )

    def read(self, slot):
        a, b, istart, jstart, w = (self.ring[self.FIELDS * slot + k] for k in range(self.FIELDS))
        return (
            a,
            b,
            pl.multiple_of(istart, self.icut),
            pl.multiple_of(jstart, self.jcut),
            w.astype(F32),
        )

    def distances(self, slot, left, right, out):
        a, b, istart, jstart, _ = self.read(slot)
        out[...] = jnp.dot(
            left[a, pl.ds(istart, self.icut), :DOT_K],
            right[b, :, pl.ds(jstart, self.jcut)],
            preferred_element_type=F32,
        )


def density_loop(group, blocks, total, left, right, mrow, acc, work):
    icut, jcut = blocks.icut, blocks.jcut
    dist, parts = work[:group], work[group:]
    zero = jnp.int32(0)
    state = (zero, zero, zero)
    for g in range(2 * group):
        state = blocks.write(g, state)
    for g in range(group):
        blocks.distances(g, left, right, dist[g])

    def step(k, state):
        for g in range(group):
            _, b, _, jstart, w = blocks.read(k * group + g)
            weight = mrow[b, :, pl.ds(jstart, jcut)] * w
            weight = jnp.concatenate([weight] * (STRIP // 8), axis=0)
            for row in range(0, icut, STRIP):
                s = jnp.maximum(dist[g][row : row + STRIP, :], TINY)
                q = s * lax.rsqrt(s)
                e = 1.0 - q
                u = jnp.maximum(e, 0.0)
                t = jnp.minimum(0.5 - (s * 3.0) * e, u * u * u) * weight
                part = t[:, :LANES]
                for at in range(1, jcut // LANES):
                    part = part + t[:, at * LANES : (at + 1) * LANES]
                parts[g][row : row + STRIP, :] = part

            state = blocks.write((k + 2) * group + g, state)
            blocks.distances((k + 1) * group + g, left, right, dist[g])
        for g in range(group):
            a, _, istart, _, _ = blocks.read(k * group + g)
            acc[a, pl.ds(istart, icut), :] += parts[g][...]
        return state

    lax.fori_loop(0, chunks(total, group), step, state)


def density_source(rows, right, mrow, at):
    right[at] = right_parts(right_comps(rows))
    mrow[at] = jnp.broadcast_to(rows[3:4], mrow.shape[1:])


def spread_left(parts, left, cell):
    for at in range(parts.shape[1] // LANES):
        left[cell, pl.ds(at * LANES, LANES), :] = parts[:, at * LANES : (at + 1) * LANES].T.astype(BF16)


def force_scales(rows):
    h = rows[4:5]
    inv = 1.0 / jnp.where(h > 0.0, h, 1.0)
    b = math.sqrt(24.0 / math.pi) * (inv * inv)
    return b, b * inv


def density_local_kernel(
    icut, jcut, group, lay, meta, own, acc, left, force_left, table, ring, right, mrow, *work
):
    slots = own.shape[2]
    ids = row_ids((8, slots))
    empty = jnp.zeros((8, slots), F32)
    for k in range(lay.cells):
        rows = own[k]
        inv = 1.0 / rows[4:5]
        comps = left_comps(rows)
        spread_left(jnp.concatenate([left_parts(comps * (inv * inv)), empty, empty], axis=0), left, k)
        scales = empty
        for at, part in enumerate(x for scale in force_scales(rows) for x in split3(scale)):
            scales = jnp.where(ids == at, part, scales)
        spread_left(jnp.concatenate([left_parts(comps), scales, empty], axis=0), force_left, k)
        density_source(rows, right, mrow, k)
        acc[k] = jnp.zeros((slots, LANES), F32)
    tiles = Tiles(icut, jcut, table)
    local_tiles(tiles, lay, meta, False)
    blocks = Blocks(tiles, ring)
    density_loop(group, blocks, tiles.blocks, left, right, mrow, acc, work)


def density_remote_kernel(
    icut, jcut, group, lay,
    meta, own, rec, rec_odd, acc_in, left, energy_in,
    rho_out, term_out, pay, odd, far, live,
    table, ring, right, mrow, acc, energy, sem, *work,
):
    cells, peers = lay.cells, lay.peers
    slots = own.shape[2]
    copy = pltpu.make_async_copy(energy_in, energy, sem)
    copy.start()
    first, face = arrivals(lay)
    ids = row_ids((8, slots))

    def receive(got, at, k):
        rows = jnp.zeros((8, slots), F32)
        for r in range(SENT):
            rows = jnp.where(ids == r, got[at, :, r * slots : (r + 1) * slots], rows)
        far[k] = rows
        density_source(rows, right, mrow, k)

    def rec_cell(k, carry):
        receive(rec, first + k, k)
        return carry

    lax.fori_loop(0, peers, rec_cell, 0, unroll=4)
    receive(rec, face, peers)
    receive(rec_odd, 0, peers + 1)
    occupied = jnp.sum(jnp.where(far[:, 3, :] > 0.0, 1.0, 0.0), axis=1, keepdims=True)
    for k in range(peers + 2):
        live[k] = occupied[k, 0].astype(jnp.int32)
    acc[...] = acc_in[...]
    tiles = Tiles(icut, jcut, table)
    remote_tiles(tiles, lay, meta, live)
    blocks = Blocks(tiles, ring)
    density_loop(group, blocks, tiles.blocks, left, right, mrow, acc, work)

    copy.wait()
    lane = lax.broadcasted_iota(jnp.int32, (1, slots), 1)
    ones = jnp.ones((8, LANES), BF16)
    for k in range(cells):
        one, two, three = split3(acc[k])
        total_row = jnp.zeros((8, slots), F32)
        for part in (three, two, one):
            total_row = total_row + lax.dot_general(
                ones, part.astype(BF16), (((1,), (1,)), ((), ())), preferred_element_type=F32
            )
        inv = 1.0 / own[k, 4:5, :]
        rho = total_row[0:1] * (16.0 / math.pi) * (inv * inv * inv)
        occupied = jnp.where(lane < meta[k], 1.0, 0.0)
        rho_out[k : k + 1, :] = rho * occupied
        term_out[k] = occupied * (GAMMA - 1.0) * energy[k : k + 1, :] / (rho + 1.0 - occupied)

    def row(cell, r):
        return term_out[cell] if r == 0 else own[cell, 3 + r : 4 + r, :]

    fill(lay, pay, odd, meta, SENT_LATER, row)


def force_source(rows, pressure, right, weights, scale, at):
    slots = rows.shape[1]
    right[at] = right_parts(right_comps(rows))
    b, c = force_scales(rows)
    scale[at] = jnp.concatenate([jnp.broadcast_to(b, (8, slots)), jnp.broadcast_to(c, (8, slots))], axis=0)
    m = rows[3:4]
    mp = m * pressure
    xv = rows[0:1] * rows[5:6] + rows[1:2] * rows[6:7] + rows[2:3] * rows[7:8]
    ids = row_ids((8, slots))
    base = jnp.where(ids == 3, 1.0, jnp.where(ids == 4, xv, rows))
    sums = jnp.concatenate([base * m, jnp.where(ids < 4, base, 0.0) * mp], axis=0)
    one, two, three = split3(sums)
    weights[at] = jnp.concatenate([one, two, three], axis=0).astype(BF16)


def force_loop(group, blocks, total, local, left, right, weights, scale, bcol, ccol, acc, work):
    icut, jcut = blocks.icut, blocks.jcut
    dist, upper, lower = work[:group], work[group : 2 * group], work[2 * group :]
    blocks.clear(group)
    for ref in (*upper, *lower):
        ref[...] = jnp.zeros_like(ref)
    zero = jnp.int32(0)
    state = (zero, zero, zero)
    for g in range(2 * group):
        state = blocks.write(group + g, state)
    for g in range(group):
        blocks.distances(group + g, left, right, dist[g])

    def sums_of(rows, columns, k, g):
        a, b, istart, jstart, w = blocks.read(k * group + g)
        adds = []
        if rows:
            wt = weights[b, :, pl.ds(jstart, jcut)]
            spec = (((1,), (1,)), ((), ()))
            part = lax.dot_general(wt, upper[g][...], spec, preferred_element_type=F32)
            part = part + lax.dot_general(wt, lower[g][...], spec, preferred_element_type=F32)
            keep = w
            if columns:
                keep = jnp.where(k * group + g < local + group, w, 0.0)
            adds.append((a, istart, part * keep))
        if columns:
            wt = weights[a, :, pl.ds(istart, icut)]
            part = jnp.dot(wt, upper[g][...], preferred_element_type=F32)
            part = part + jnp.dot(wt, lower[g][...], preferred_element_type=F32)
            adds.append((b, jstart, part * w))
        return adds

    def store(adds):
        for cell, start, part in adds:
            acc[cell, :, pl.ds(start, part.shape[1])] += part

    def step(rows, columns, k, state):
        adds = []
        for g in range(group):
            adds += sums_of(rows, columns, k, g)

            a, b, istart, jstart, _ = blocks.read((k + 1) * group + g)
            bj = jnp.concatenate([scale[b, 0:8, pl.ds(jstart, jcut)]] * (STRIP // 8), axis=0)
            cj = jnp.concatenate([scale[b, 8:16, pl.ds(jstart, jcut)]] * (STRIP // 8), axis=0)
            for row in range(0, icut, STRIP):
                s = jnp.maximum(dist[g][row : row + STRIP, :], TINY)
                r = lax.rsqrt(s)
                d = s * r
                bi = bcol[a, pl.ds(istart + row, STRIP), :]
                ci = ccol[a, pl.ds(istart + row, STRIP), :]
                bi = jnp.concatenate([bi] * (jcut // LANES), axis=1)
                ci = jnp.concatenate([ci] * (jcut // LANES), axis=1)
                t = ci * d
                u = jnp.maximum(bi - t, 0.0)
                v = jnp.minimum(t, u)
                slope = (u + u - v) * v
                t = cj * d
                u = jnp.maximum(bj - t, 0.0)
                v = jnp.minimum(t, u)
                slope = (slope + (u + u - v) * v) * r
                rounded = slope.astype(BF16)
                upper[g][row : row + STRIP, :] = rounded
                lower[g][row : row + STRIP, :] = (slope - rounded.astype(F32)).astype(BF16)

            state = blocks.write((k + 3) * group + g, state)
            blocks.distances((k + 2) * group + g, left, right, dist[g])
        store(adds)
        return state

    steps = chunks(total, group)
    adds = []
    if local is None:
        lax.fori_loop(0, steps, functools.partial(step, True, False), state)
        for g in range(group):
            adds += sums_of(True, False, steps, g)
    else:
        first = jnp.minimum(chunks(local, group) + 1, steps)
        state = lax.fori_loop(0, first, functools.partial(step, True, True), state)
        lax.fori_loop(first, steps, functools.partial(step, False, True), state)
        for g in range(group):
            adds += sums_of(True, True, steps, g)
    store(adds)


def force_local_kernel(
    icut, jcut, group, lay,
    meta, own, term, left,
    acc_out, bcol, ccol,
    table, ring, right, weights, scale, acc, *work,
):
    slots = own.shape[2]
    part = lax.broadcasted_iota(jnp.int32, (COLS, 2 * LANES), 0) - DOT_K
    lane = lax.broadcasted_iota(jnp.int32, (COLS, 2 * LANES), 1)
    of_b = (part >= 0) & (part < 3) & (lane < LANES)
    of_c = (part >= 3) & (part < 6) & (lane >= LANES)
    pick = jnp.where(of_b | of_c, 1.0, 0.0).astype(BF16)
    for k in range(lay.cells):
        force_source(own[k], term[k], right, weights, scale, k)
        acc[k] = jnp.zeros((DOT_K, slots), F32)
        for at in range(slots // LANES):
            here = pl.ds(at * LANES, LANES)
            both = jnp.dot(left[k, here, :], pick, preferred_element_type=F32)
            bcol[k, here, :] = both[:, :LANES]
            ccol[k, here, :] = both[:, LANES:]
    tiles = Tiles(icut, jcut, table)
    local = local_tiles(tiles, lay, meta, True)
    blocks = Blocks(tiles, ring)
    force_loop(
        group, blocks, tiles.blocks, local, left, right, weights, scale, bcol, ccol, acc, work
    )
    for k in range(lay.cells):
        acc_out[k] = acc[k, 0:16, :] + (acc[k, 16:32, :] + acc[k, 32:48, :])


def force_remote_kernel(
    icut, jcut, group, lay,
    meta, live, own, far, term, rterm, odd_term, acc_in, left, bcol, ccol,
    accel_out, heat_out,
    table, ring, right, weights, scale, acc, *work,
):
    cells, peers = lay.cells, lay.peers
    slots = own.shape[2]
    first, face = arrivals(lay)
    ids = row_ids((8, slots))

    def receive(got, at, k):
        rows = far[k]
        for r in range(1, SENT_LATER):
            rows = jnp.where(ids == 3 + r, got[at, :, r * slots : (r + 1) * slots], rows)
        force_source(rows, got[at, :, :slots], right, weights, scale, k)

    def rec_cell(k, carry):
        receive(rterm, first + k, k)
        return carry

    lax.fori_loop(0, peers, rec_cell, 0, unroll=4)
    receive(rterm, face, peers)
    receive(odd_term, 0, peers + 1)
    acc[...] = jnp.zeros_like(acc)
    tiles = Tiles(icut, jcut, table)
    remote_tiles(tiles, lay, meta, live)
    blocks = Blocks(tiles, ring)
    force_loop(
        group, blocks, tiles.blocks, None, left, right, weights, scale, bcol, ccol, acc, work
    )

    lane = lax.broadcasted_iota(jnp.int32, (1, slots), 1)
    for k in range(cells):
        occupied = jnp.where(lane < meta[k], 1.0, 0.0)
        sums = acc_in[k] + acc[k, 0:16, :] + (acc[k, 16:32, :] + acc[k, 32:48, :])
        pressure = term[k]
        x = [own[k, d : d + 1, :] for d in range(3)]
        v = [own[k, 5 + d : 6 + d, :] for d in range(3)]
        both = pressure * sums[3:4] + sums[11:12]
        for d in range(3):
            accel_out[d, k : k + 1, :] = occupied * (
                x[d] * both - pressure * sums[d : d + 1] - sums[8 + d : 9 + d]
            )
        xv = x[0] * v[0] + x[1] * v[1] + x[2] * v[2]
        total_heat = xv * sums[3:4] + sums[4:5]
        for d in range(3):
            total_heat = total_heat - v[d] * sums[d : d + 1] - x[d] * sums[5 + d : 6 + d]
        heat_out[k : k + 1, :] = -occupied * pressure * total_heat


def on_device(positions, velocities, mass, smoothing, energy, counts, send, pairs, edge):
    cells, slots = mass.shape
    peers = send.shape[2]
    regions = 2 * lax.axis_size("pair")
    lay = Meta(cells, peers, pairs.shape[2])
    others = peers + 2
    most = max(cells * (cells - 1) // 2 + 3 * cells, cells * cells, others) + 1
    icut, jcut, group = 128, slots // 2, 8
    ring = Blocks.FIELDS * (most * (slots // icut) * (slots // jcut) + 6 * group)
    shape = jax.ShapeDtypeStruct
    params = pltpu.CompilerParams(vmem_limit_bytes=20 * 1024 * 1024)
    send = send.reshape(peers)
    pairs = jnp.transpose(pairs, (0, 1, 3, 2))
    integers = (counts, send, pairs, edge)
    floats = (positions, velocities, mass, smoothing)
    integers, floats, energy = jax.tree.map(
        lambda x: pltpu.with_memory_space_constraint(x, pltpu.HBM), (integers, floats, energy)
    )
    lists = [pltpu.SMEM((Tiles.FIELDS * most,), jnp.int32), pltpu.SMEM((ring,), jnp.int32)]
    density_work = [pltpu.VMEM((icut, jcut), F32)] * group + [pltpu.VMEM((icut, LANES), F32)] * group
    force_work = [pltpu.VMEM((icut, jcut), F32)] * group + [pltpu.VMEM((icut, jcut), BF16)] * (2 * group)
    wide = shape((cells, slots, LANES), F32)
    left_shape = shape((cells, slots, COLS), BF16)
    weight_shape = lambda count: pltpu.VMEM((count, DOT_K, slots), BF16)

    def exchange(pay, odd):
        between = [(r, r + 1) for r in range(1, regions - 1, 2)]
        swap = between + [(b, a) for a, b in between]
        got_odd = lax.ppermute(odd, ("pair", "side"), swap)
        return lax.all_to_all(pay, ("side", "cell"), split_axis=0, concat_axis=0, tiled=True), got_odd

    own, pay, odd, meta = pl.pallas_call(
        functools.partial(prep_kernel, lay),
        out_shape=[
            shape((cells, ROWS, slots), F32),
            shape((2 * peers, 1, SENT * slots), F32),
            shape((1, 1, SENT * slots), F32),
            shape((lay.size,), jnp.int32),
        ],
        in_specs=[HBM] * 8,
        out_specs=[VMEM] * 3 + [SMEM],
        scratch_shapes=[pltpu.SMEM(x.shape, jnp.int32) for x in integers]
        + [pltpu.VMEM(x.shape, F32) for x in floats]
        + [pltpu.SemaphoreType.DMA((8,))],
        compiler_params=params,
        name="prep",
    )(*integers, *floats)

    rec, rec_odd = exchange(pay, odd)

    acc, left, force_left = pl.pallas_call(
        functools.partial(density_local_kernel, icut, jcut, group, lay),
        out_shape=[wide, left_shape, left_shape],
        in_specs=[SMEM, VMEM],
        out_specs=[VMEM] * 3,
        scratch_shapes=lists + [weight_shape(cells), pltpu.VMEM((cells, 8, slots), F32)] + density_work,
        compiler_params=params,
        name="density_local",
    )(meta, own)

    density, term, pay, odd, far, live = pl.pallas_call(
        functools.partial(density_remote_kernel, icut, jcut, group, lay),
        out_shape=[
            shape((cells, slots), F32),
            shape((cells, 1, slots), F32),
            shape((2 * peers, 1, SENT_LATER * slots), F32),
            shape((1, 1, SENT_LATER * slots), F32),
            shape((others, ROWS, slots), F32),
            shape((others,), jnp.int32),
        ],
        in_specs=[SMEM] + [VMEM] * 5 + [HBM],
        out_specs=[VMEM] * 5 + [SMEM],
        scratch_shapes=lists
        + [
            weight_shape(others),
            pltpu.VMEM((others, 8, slots), F32),
            pltpu.VMEM((cells, slots, LANES), F32),
            pltpu.VMEM(energy.shape, F32),
            pltpu.SemaphoreType.DMA,
        ]
        + density_work,
        compiler_params=params,
        name="density_remote",
    )(meta, own, rec, rec_odd, acc, left, energy)

    rterm, odd_term = exchange(pay, odd)

    acc, bcol, ccol = pl.pallas_call(
        functools.partial(force_local_kernel, icut, jcut, group, lay),
        out_shape=[shape((cells, 16, slots), F32), wide, wide],
        in_specs=[SMEM] + [VMEM] * 3,
        out_specs=[VMEM] * 3,
        scratch_shapes=lists
        + [
            weight_shape(cells),
            weight_shape(cells),
            pltpu.VMEM((cells, 16, slots), F32),
            pltpu.VMEM((cells, DOT_K, slots), F32),
        ]
        + force_work,
        compiler_params=params,
        name="force_local",
    )(meta, own, term, force_left)

    accel, heat = pl.pallas_call(
        functools.partial(force_remote_kernel, icut, jcut, group, lay),
        out_shape=[shape((3, cells, slots), F32), shape((cells, slots), F32)],
        in_specs=[SMEM] * 2 + [VMEM] * 9,
        out_specs=[VMEM] * 2,
        scratch_shapes=lists
        + [
            weight_shape(others),
            weight_shape(others),
            pltpu.VMEM((others, 16, slots), F32),
            pltpu.VMEM((cells, DOT_K, slots), F32),
        ]
        + force_work,
        compiler_params=params,
        name="force_remote",
    )(meta, live, own, far, term, rterm, odd_term, acc, force_left, bcol, ccol)
    return density, accel, heat


def solution(mesh):
    regions, peers = mesh.devices.shape
    mesh = jax.sharding.Mesh(mesh.devices.reshape(regions // 2, 2, peers), ("pair", "side", "cell"))
    region = ("pair", "side")
    every = (*region, "cell")
    placed = (
        P(None, every, None),
        P(None, every, None),
        P(every, None),
        P(every, None),
        P(every, None),
        P(every),
        P(region, "cell", None, None),
        P(region, "cell", None, None),
        P(region, "cell", None),
    )
    return jax.shard_map(
        on_device,
        mesh=mesh,
        in_specs=placed,
        out_specs=(P(every, None), P(None, every, None), P(every, None)),
        check_vma=False,
    )
```

profile of v0, /device:TPU:9, one launch (start us, length us, event | category | flops | bytes accessed | tf_op | source)
XLA Modules:
  0.0 46.3 jit_solution(7542195408857561277)
XLA Ops:
  0.6 1.6 %prep.1 = (f32[4,8,512]{2,1,0:T(8,128)S(1)}, f32[16,1,2048]{2,1,0:T(1,128)}, f32[1,1,2048]{2,1,0:T(1,128)S(1)}, s32[22]{0:T(128)S(1)}) custom-call(s32[4]{0:T(128)} %counts_in.1, s32[8]{0:T(128)} %bitcast.3, s32[1,1,2,4]{3,2,1,0:T(2,128)} %bitcast.2, s32[1,1,2]{2,1,0:T(1,128)} %edge_in.1, f32[3,4,512]{2,1,0:T(4,128)} %pos_in.1, f32[3,4,512]{2,1,0:T(4,128)} %vel_in.1, ...), custom_call_target="tpu_custom_call" | custom-call | tf_op jit(solution)/shard_map/prep/pallas_call | solution.py:607
  2.2 5.5 %all-to-all-start = ((f32[16,1,2048]{2,1,0:T(1,128)}), f32[16,1,2048]{2,1,0:T(1,128)S(1)}, u32[]{:S(2)}, u32[]{:S(2)}) async-start(f32[16,1,2048]{2,1,0:T(1,128)} %get-tuple-element.23), calls=%async_computation | async-start | bytes 262144 | tf_op jit(solution)/shard_map/all_to_all | solution.py:605
  7.8 3.1 %collective-permute-start = (f32[1,1,2048]{2,1,0:T(1,128)S(1)}, f32[1,1,2048]{2,1,0:T(1,128)S(1)}, u32[]{:S(2)}, u32[]{:S(2)}) collective-permute-start(f32[1,1,2048]{2,1,0:T(1,128)S(1)} %get-tuple-element.24), channel_id=1, source_target_pairs={{8,16},{16,8},{9,17},{17,9},{10,18},{18,10},{11,19},{19,11},{12,20... | collective-permute-start | bytes 24584 | tf_op jit(solution)/shard_map/ppermute | solution.py:604
  10.9 8.3 %density_local.1 = (f32[4,512,128]{2,1,0:T(8,128)S(1)}, bf16[4,512,64]{2,1,0:T(8,128)(2,1)S(1)}, bf16[4,512,64]{2,1,0:T(8,128)(2,1)S(1)}) custom-call(s32[22]{0:T(128)S(1)} %get-tuple-element.21.meta, f32[4,8,512]{2,1,0:T(8,128)S(1)} %get-tuple-element.22.own), custom_call_target="tpu_custom_call" | custom-call | tf_op jit(solution)/shard_map/density_local/pallas_call | solution.py:626
  19.2 0.0 collective-permute-done.rec_odd
  19.2 0.0 all-to-all-done.rec
  19.2 5.4 %density_remote.1 = (f32[4,512]{1,0:T(4,128)}, f32[4,1,512]{2,1,0:T(1,128)S(1)}, f32[16,1,2560]{2,1,0:T(1,128)}, f32[1,1,2560]{2,1,0:T(1,128)S(1)}, f32[10,8,512]{2,1,0:T(8,128)S(1)}, /*index=5*/s32[10]{0:T(128)S(1)}) custom-call(s32[22]{0:T(128)S(1)} %get-tuple-element.21.meta, f32[4,8,512]{2,1,0:T(8,128)S(1)} %get-tuple-element.22.own, ...), custom_call_target="tpu_custom_call" | custom-call | tf_op jit(solution)/shard_map/density_remote/pallas_call | solution.py:636
  24.6 3.4 %all-to-all-start.1 = ((f32[16,1,2560]{2,1,0:T(1,128)}), f32[16,1,2560]{2,1,0:T(1,128)S(1)}, u32[]{:S(2)}, u32[]{:S(2)}) async-start(f32[16,1,2560]{2,1,0:T(1,128)} %get-tuple-element.31), calls=%async_computation.1 | async-start | bytes 327680 | tf_op jit(solution)/shard_map/all_to_all | solution.py:605
  28.1 1.9 %collective-permute-start.1 = (f32[1,1,2560]{2,1,0:T(1,128)S(1)}, f32[1,1,2560]{2,1,0:T(1,128)S(1)}, u32[]{:S(2)}, u32[]{:S(2)}) collective-permute-start(f32[1,1,2560]{2,1,0:T(1,128)S(1)} %get-tuple-element.32), channel_id=1, source_target_pairs={{8,16},{16,8},{9,17},{17,9},{10,18},{18,10},{11,19},{19,11},{12,20... | collective-permute-start | bytes 30728 | tf_op jit(solution)/shard_map/ppermute | solution.py:604
  30.0 9.0 %force_local.1 = (f32[4,16,512]{2,1,0:T(8,128)S(1)}, f32[4,512,128]{2,1,0:T(8,128)S(1)}, f32[4,512,128]{2,1,0:T(8,128)S(1)}) custom-call(s32[22]{0:T(128)S(1)} %get-tuple-element.21.meta, f32[4,8,512]{2,1,0:T(8,128)S(1)} %get-tuple-element.22.own, f32[4,1,512]{2,1,0:T(1,128)S(1)} %get-tuple-element.30.term, bf16[4,512,64]{2,1,0:T(8,128)(2,1)S(1)} %get-tuple-element.33.left), custom_call_target="tpu_custom_call" | custom-call | tf_op jit(solution)/shard_map/force_local/pallas_call | solution.py:663
  39.0 0.0 collective-permute-done.1.odd_term
  39.0 0.0 all-to-all-done.1.rterm
  39.0 7.3 %force_remote.1 = (f32[3,4,512]{2,1,0:T(4,128)}, f32[4,512]{1,0:T(4,128)}) custom-call(s32[22]{0:T(128)S(1)} %get-tuple-element.21.meta, s32[10]{0:T(128)S(1)} %get-tuple-element.28.live, f32[4,8,512]{2,1,0:T(8,128)S(1)} %get-tuple-element.22.own, f32[10,8,512]{2,1,0:T(8,128)S(1)} %get-tuple-element.29.far, f32[4,1,512]{2,1,0:T(1,128)S(1)} %get-tuple-element.30.term, ...), custom_call_target="tpu_custom_call" | custom-call | tf_op jit(solution)/shard_map/force_remote/pallas_call | solution.py:680
Async XLA Ops:
  2.2 16.9 %all-to-all-start = ((f32[16,1,2048]{2,1,0:T(1,128)}), f32[16,1,2048]{2,1,0:T(1,128)S(1)}, u32[]{:S(2)}, u32[]{:S(2)}) async-start(f32[16,1,2048]{2,1,0:T(1,128)} %get-tuple-element.23), calls=%async_computation | async-start | bytes 262144 | tf_op jit(solution)/shard_map/all_to_all | solution.py:605
  7.8 11.4 %collective-permute-start = (f32[1,1,2048]{2,1,0:T(1,128)S(1)}, f32[1,1,2048]{2,1,0:T(1,128)S(1)}, u32[]{:S(2)}, u32[]{:S(2)}) collective-permute-start(f32[1,1,2048]{2,1,0:T(1,128)S(1)} %get-tuple-element.24), channel_id=1, source_target_pairs={{8,16},{16,8},{9,17},{17,9},{10,18},{18,10},{11,19},{19,11},{12,20... | collective-permute-start | bytes 24584 | tf_op jit(solution)/shard_map/ppermute | solution.py:604
  24.6 14.4 %all-to-all-start.1 = ((f32[16,1,2560]{2,1,0:T(1,128)}), f32[16,1,2560]{2,1,0:T(1,128)S(1)}, u32[]{:S(2)}, u32[]{:S(2)}) async-start(f32[16,1,2560]{2,1,0:T(1,128)} %get-tuple-element.31), calls=%async_computation.1 | async-start | bytes 327680 | tf_op jit(solution)/shard_map/all_to_all | solution.py:605
  28.1 10.9 %collective-permute-start.1 = (f32[1,1,2560]{2,1,0:T(1,128)S(1)}, f32[1,1,2560]{2,1,0:T(1,128)S(1)}, u32[]{:S(2)}, u32[]{:S(2)}) collective-permute-start(f32[1,1,2560]{2,1,0:T(1,128)S(1)} %get-tuple-element.32), channel_id=1, source_target_pairs={{8,16},{16,8},{9,17},{17,9},{10,18},{18,10},{11,19},{19,11},{12,20... | collective-permute-start | bytes 30728 | tf_op jit(solution)/shard_map/ppermute | solution.py:604
where the time goes:
time: 47 us; the launch traced here: 46.3 us
  Pallas kernels  31.6 us (67%)
  starting transfers between devices  14 us (30%)
  between operations  0.72 us (2%)
    pallas_call x1, Pallas kernels, on_device(): pl.pallas_call(functools.partial(force_local_kernel, icut, jcut, group, l...  8.98 us
    all_to_all x2, starting transfers between devices, exchange(): lax.all_to_all(pay, ('side', 'cell'), split_axis=0, concat_axis=0, tiled=...  8.95 us
    pallas_call x1, Pallas kernels, on_device(): pl.pallas_call(functools.partial(density_local_kernel, icut, jcut, group,...  8.25 us
    pallas_call x1, Pallas kernels, on_device(): pl.pallas_call(functools.partial(force_remote_kernel, icut, jcut, group,...  7.3 us
    pallas_call x1, Pallas kernels, on_device(): pl.pallas_call(functools.partial(density_remote_kernel, icut, jcut, group...  5.43 us
    ppermute x2, starting transfers between devices, exchange(): got_odd = lax.ppermute(odd, ('pair', 'side'), swap)  5.05 us
    pallas_call x1, Pallas kernels, on_device(): pl.pallas_call(functools.partial(prep_kernel, lay), out_shape=[shape((cel...  1.6 us
  transfers between devices with their start and end apart: 4, of which 0 were waited for; matrix products, arithmetic and copies ran while one was open for 0% of the time, Pallas kernels for 37%

commit v1 on v0

--- a/solution.py
+++ b/solution.py
@@ -18,8 +18,6 @@
 DOT_K = 48
 COLS = 64
 STRIP = 16
-SENT = 4
-SENT_LATER = 5
 
 VMEM = pl.BlockSpec(memory_space=pltpu.VMEM)
 SMEM = pl.BlockSpec(memory_space=pltpu.SMEM)
@@ -66,8 +64,8 @@
 
 
 class Meta:
-    def __init__(self, cells, peers, pairs):
-        self.cells, self.peers, self.pairs = cells, peers, pairs
+    def __init__(self, cells, regions, peers, pairs):
+        self.cells, self.regions, self.peers, self.pairs = cells, regions, peers, pairs
         self.send = cells
         self.pair = cells + peers
         self.edge = self.pair + 2 * pairs
@@ -111,38 +109,34 @@
         own[k, 3:4, :] = jnp.where(live, mass[k : k + 1, :], 0.0)
         own[k, 4:5, :] = smooth[k : k + 1, :]
 
-    def row(cell, r):
-        return own[cell, r : r + 1, :]
-
-    fill(lay, pay, odd, meta, SENT, row)
-
-
-def fill(lay, pay, odd, meta, count, row):
-    slots = pay.shape[2] // count
-    side = lax.axis_index("side")
-    first = side * lay.peers
+    place = Place(lay)
     pay[...] = jnp.zeros_like(pay)
 
-    def put(out, at, cell, keep):
-        for r in range(count):
-            value = row(cell, r)
-            if keep is not None:
-                value = jnp.where(keep, value, 0.0)
-            out[at, :, r * slots : (r + 1) * slots] = value
-
     def peer(k, carry):
-        picked = meta[lay.send + k]
-        put(pay, first + k, jnp.maximum(picked, 0), picked >= 0)
+        picked = send[k]
+        pay[place.pair_peers + k] = jnp.where(picked >= 0, own[jnp.maximum(picked, 0)], 0.0)
         return carry
 
     lax.fori_loop(0, lay.peers, peer, 0)
-    put(pay, lay.peers - first + lax.axis_index("cell"), meta[lay.edge + 1 - side], None)
-    put(odd, 0, meta[lay.edge + side], None)
-
-
-def arrivals(lay):
-    first = lax.axis_index("side") * lay.peers
-    return first, lay.peers - first + lax.axis_index("cell")
+    pay[place.pair_partner] = own[meta[place.partner_edge]]
+    odd[0] = own[meta[place.odd_edge]]
+
+
+class Place:
+    def __init__(self, lay):
+        peers, regions = lay.peers, lay.regions
+        self.side = lax.axis_index("side")
+        here = lax.axis_index("cell")
+        region = 2 * lax.axis_index("pair") + self.side
+        other = region - 1 + 2 * self.side
+        self.partner_edge = lay.edge + 1 - self.side
+        self.odd_edge = lay.edge + self.side
+        self.pair_peers = self.side * peers
+        self.pair_partner = (1 - self.side) * peers + here
+        self.peers = region * peers
+        self.partner = (region + 1 - 2 * self.side) * peers + here
+        self.has_odd = (other >= 0) & (other < regions)
+        self.odd = jnp.clip(other, 0, regions - 1) * peers + here
 
 
 class Tiles:
@@ -207,9 +201,9 @@
         picked = meta[lay.send + k]
         a = jnp.maximum(picked, 0)
         tiles.whole(a, k, one, (picked >= 0) & (live[k] > 0), meta[a], live[k])
-    side = lax.axis_index("side")
-    for b, edge in ((lay.peers, 1 - side), (lay.peers + 1, side)):
-        a = meta[lay.edge + edge]
+    place = Place(lay)
+    for b, edge in ((lay.peers, place.partner_edge), (lay.peers + 1, place.odd_edge)):
+        a = meta[edge]
         tiles.whole(a, b, one, live[b] > 0, meta[a], live[b])
     tiles.close()
 
@@ -338,33 +332,28 @@
 def density_remote_kernel(
     icut, jcut, group, lay,
     meta, own, rec, rec_odd, acc_in, left, energy_in,
-    rho_out, term_out, pay, odd, far, live,
+    rho_out, term_out, pay, live,
     table, ring, right, mrow, acc, energy, sem, *work,
 ):
     cells, peers = lay.cells, lay.peers
     slots = own.shape[2]
     copy = pltpu.make_async_copy(energy_in, energy, sem)
     copy.start()
-    first, face = arrivals(lay)
-    ids = row_ids((8, slots))
-
-    def receive(got, at, k):
-        rows = jnp.zeros((8, slots), F32)
-        for r in range(SENT):
-            rows = jnp.where(ids == r, got[at, :, r * slots : (r + 1) * slots], rows)
-        far[k] = rows
-        density_source(rows, right, mrow, k)
+    place = Place(lay)
+    occupied = jnp.where(rec[:, 3, :] > 0.0, 1.0, 0.0).reshape(2, peers, slots)
+    occupied = jnp.sum(jnp.where(place.side == 0, occupied[0], occupied[1]), axis=1, keepdims=True)
+    for k in range(peers):
+        live[k] = occupied[k, 0].astype(jnp.int32)
+    for k, rows in ((peers, rec[place.pair_partner]), (peers + 1, rec_odd[0])):
+        live[k] = jnp.sum(jnp.where(rows[3:4] > 0.0, 1.0, 0.0)).astype(jnp.int32)
 
     def rec_cell(k, carry):
-        receive(rec, first + k, k)
+        density_source(rec[place.pair_peers + k], right, mrow, k)
         return carry
 
     lax.fori_loop(0, peers, rec_cell, 0, unroll=4)
-    receive(rec, face, peers)
-    receive(rec_odd, 0, peers + 1)
-    occupied = jnp.sum(jnp.where(far[:, 3, :] > 0.0, 1.0, 0.0), axis=1, keepdims=True)
-    for k in range(peers + 2):
-        live[k] = occupied[k, 0].astype(jnp.int32)
+    density_source(rec[place.pair_partner], right, mrow, peers)
+    density_source(rec_odd[0], right, mrow, peers + 1)
     acc[...] = acc_in[...]
     tiles = Tiles(icut, jcut, table)
     remote_tiles(tiles, lay, meta, live)
@@ -387,10 +376,18 @@
         rho_out[k : k + 1, :] = rho * occupied
         term_out[k] = occupied * (GAMMA - 1.0) * energy[k : k + 1, :] / (rho + 1.0 - occupied)
 
-    def row(cell, r):
-        return term_out[cell] if r == 0 else own[cell, 3 + r : 4 + r, :]
-
-    fill(lay, pay, odd, meta, SENT_LATER, row)
+    pay[...] = jnp.zeros_like(pay)
+
+    def peer(k, carry):
+        pay[place.peers + k] = term_out[jnp.maximum(meta[lay.send + k], 0)]
+        return carry
+
+    lax.fori_loop(0, peers, peer, 0)
+    pay[place.partner] = term_out[meta[place.partner_edge]]
+
+    @pl.when(place.has_odd)
+    def _():
+        pay[place.odd] = term_out[meta[place.odd_edge]]
 
 
 def force_source(rows, pressure, right, weights, scale, at):
@@ -524,28 +521,21 @@
 
 def force_remote_kernel(
     icut, jcut, group, lay,
-    meta, live, own, far, term, rterm, odd_term, acc_in, left, bcol, ccol,
+    meta, live, own, rec, rec_odd, term, rterm, acc_in, left, bcol, ccol,
     accel_out, heat_out,
     table, ring, right, weights, scale, acc, *work,
 ):
     cells, peers = lay.cells, lay.peers
     slots = own.shape[2]
-    first, face = arrivals(lay)
-    ids = row_ids((8, slots))
-
-    def receive(got, at, k):
-        rows = far[k]
-        for r in range(1, SENT_LATER):
-            rows = jnp.where(ids == 3 + r, got[at, :, r * slots : (r + 1) * slots], rows)
-        force_source(rows, got[at, :, :slots], right, weights, scale, k)
+    place = Place(lay)
 
     def rec_cell(k, carry):
-        receive(rterm, first + k, k)
+        force_source(rec[place.pair_peers + k], rterm[place.peers + k], right, weights, scale, k)
         return carry
 
     lax.fori_loop(0, peers, rec_cell, 0, unroll=4)
-    receive(rterm, face, peers)
-    receive(odd_term, 0, peers + 1)
+    force_source(rec[place.pair_partner], rterm[place.partner], right, weights, scale, peers)
+    force_source(rec_odd[0], rterm[place.odd], right, weights, scale, peers + 1)
     acc[...] = jnp.zeros_like(acc)
     tiles = Tiles(icut, jcut, table)
     remote_tiles(tiles, lay, meta, live)
@@ -577,7 +567,7 @@
     cells, slots = mass.shape
     peers = send.shape[2]
     regions = 2 * lax.axis_size("pair")
-    lay = Meta(cells, peers, pairs.shape[2])
+    lay = Meta(cells, regions, peers, pairs.shape[2])
     others = peers + 2
     most = max(cells * (cells - 1) // 2 + 3 * cells, cells * cells, others) + 1
     icut, jcut, group = 128, slots // 2, 8
@@ -598,18 +588,12 @@
     left_shape = shape((cells, slots, COLS), BF16)
     weight_shape = lambda count: pltpu.VMEM((count, DOT_K, slots), BF16)
 
-    def exchange(pay, odd):
-        between = [(r, r + 1) for r in range(1, regions - 1, 2)]
-        swap = between + [(b, a) for a, b in between]
-        got_odd = lax.ppermute(odd, ("pair", "side"), swap)
-        return lax.all_to_all(pay, ("side", "cell"), split_axis=0, concat_axis=0, tiled=True), got_odd
-
     own, pay, odd, meta = pl.pallas_call(
         functools.partial(prep_kernel, lay),
         out_shape=[
             shape((cells, ROWS, slots), F32),
-            shape((2 * peers, 1, SENT * slots), F32),
-            shape((1, 1, SENT * slots), F32),
+            shape((2 * peers, ROWS, slots), F32),
+            shape((1, ROWS, slots), F32),
             shape((lay.size,), jnp.int32),
         ],
         in_specs=[HBM] * 8,
@@ -621,7 +605,10 @@
         name="prep",
     )(*integers, *floats)
 
-    rec, rec_odd = exchange(pay, odd)
+    between = [(r, r + 1) for r in range(1, regions - 1, 2)]
+    swap = between + [(b, a) for a, b in between]
+    rec_odd = lax.ppermute(odd, ("pair", "side"), swap)
+    rec = lax.all_to_all(pay, ("side", "cell"), split_axis=0, concat_axis=0, tiled=True)
 
     acc, left, force_left = pl.pallas_call(
         functools.partial(density_local_kernel, icut, jcut, group, lay),
@@ -633,18 +620,16 @@
         name="density_local",
     )(meta, own)
 
-    density, term, pay, odd, far, live = pl.pallas_call(
+    density, term, pay, live = pl.pallas_call(
         functools.partial(density_remote_kernel, icut, jcut, group, lay),
         out_shape=[
             shape((cells, slots), F32),
             shape((cells, 1, slots), F32),
-            shape((2 * peers, 1, SENT_LATER * slots), F32),
-            shape((1, 1, SENT_LATER * slots), F32),
-            shape((others, ROWS, slots), F32),
+            shape((regions * peers, 1, slots), F32),
             shape((others,), jnp.int32),
         ],
         in_specs=[SMEM] + [VMEM] * 5 + [HBM],
-        out_specs=[VMEM] * 5 + [SMEM],
+        out_specs=[VMEM] * 3 + [SMEM],
         scratch_shapes=lists
         + [
             weight_shape(others),
@@ -658,7 +643,7 @@
         name="density_remote",
     )(meta, own, rec, rec_odd, acc, left, energy)
 
-    rterm, odd_term = exchange(pay, odd)
+    rterm = lax.all_to_all(pay, ("pair", "side", "cell"), split_axis=0, concat_axis=0, tiled=True)
 
     acc, bcol, ccol = pl.pallas_call(
         functools.partial(force_local_kernel, icut, jcut, group, lay),
@@ -692,7 +677,7 @@
         + force_work,
         compiler_params=params,
         name="force_remote",
-    )(meta, live, own, far, term, rterm, odd_term, acc, force_left, bcol, ccol)
+    )(meta, live, own, rec, rec_odd, term, rterm, acc, force_left, bcol, ccol)
     return density, accel, heat
 
 

time: 47 us -> 44.8 us (0.953)
  the two profiles are of different devices: /device:TPU:9 before, /device:TPU:19 now
where the time goes in v1:
time: 44.8 us; the launch traced here: 45.1 us
  Pallas kernels  33.1 us (74%)
  starting transfers between devices  11.3 us (25%)
  between operations  0.7 us (2%)
    pallas_call x1, Pallas kernels, on_device(): pl.pallas_call(functools.partial(force_local_kernel, icut, jcut, group, l...  8.95 us
    pallas_call x1, Pallas kernels, on_device(): pl.pallas_call(functools.partial(force_remote_kernel, icut, jcut, group,...  8.29 us
    pallas_call x1, Pallas kernels, on_device(): pl.pallas_call(functools.partial(density_local_kernel, icut, jcut, group,...  8.25 us
    pallas_call x1, Pallas kernels, on_device(): pl.pallas_call(functools.partial(density_remote_kernel, icut, jcut, group...  5.97 us
    all_to_all x1, starting transfers between devices, on_device(): lax.all_to_all(pay, ('side', 'cell'), split_axis=0, concat_axis=0, tiled=...  5.61 us
    all_to_all x1, starting transfers between devices, on_device(): lax.all_to_all(pay, ('pair', 'side', 'cell'), split_axis=0, concat_axis=0...  3.7 us
    ppermute x1, starting transfers between devices, on_device(): rec_odd = lax.ppermute(odd, ('pair', 'side'), swap)  1.96 us
    pallas_call x1, Pallas kernels, on_device(): pl.pallas_call(functools.partial(prep_kernel, lay), out_shape=[shape((cel...  1.65 us
  transfers between devices with their start and end apart: 3, of which 0 were waited for; matrix products, arithmetic and copies ran while one was open for 0% of the time, Pallas kernels for 38%

profile of v1, /device:TPU:19, one launch (start us, length us, event | category | flops | bytes accessed | tf_op | source)
XLA Modules:
  0.0 45.1 jit_solution(17501939943024313657)
XLA Ops:
  0.6 1.6 %prep.1 = (f32[4,8,512]{2,1,0:T(8,128)S(1)}, f32[16,8,512]{2,1,0:T(8,128)}, f32[1,8,512]{2,1,0:T(8,128)S(1)}, s32[22]{0:T(128)S(1)}) custom-call(s32[4]{0:T(128)} %counts_in.1, s32[8]{0:T(128)} %bitcast.3, s32[1,1,2,4]{3,2,1,0:T(2,128)} %bitcast.2, s32[1,1,2]{2,1,0:T(1,128)} %edge_in.1, f32[3,4,512]{2,1,0:T(4,128)} %pos_in.1, f32[3,4,512]{2,1,0:T(4,128)} %vel_in.1, ...), custom_call_target="tpu_custom_call" | custom-call | tf_op jit(solution)/shard_map/prep/pallas_call | solution.py:591
  2.3 5.6 %all-to-all-start = ((f32[16,8,512]{2,1,0:T(8,128)}), f32[16,8,512]{2,1,0:T(8,128)S(1)}, u32[]{:S(2)}, u32[]{:S(2)}) async-start(f32[16,8,512]{2,1,0:T(8,128)} %get-tuple-element.21), calls=%async_computation | async-start | bytes 524288 | tf_op jit(solution)/shard_map/all_to_all | solution.py:611
  7.9 2.0 %collective-permute-start = (f32[1,8,512]{2,1,0:T(8,128)S(1)}, f32[1,8,512]{2,1,0:T(8,128)S(1)}, u32[]{:S(2)}, u32[]{:S(2)}) collective-permute-start(f32[1,8,512]{2,1,0:T(8,128)S(1)} %get-tuple-element.22), channel_id=1, source_target_pairs={{8,16},{16,8},{9,17},{17,9},{10,18},{18,10},{11,19},{19,11},{12,20... | collective-permute-start | bytes 49160 | tf_op jit(solution)/shard_map/ppermute | solution.py:610
  9.9 8.3 %density_local.1 = (f32[4,512,128]{2,1,0:T(8,128)S(1)}, bf16[4,512,64]{2,1,0:T(8,128)(2,1)S(1)}, bf16[4,512,64]{2,1,0:T(8,128)(2,1)S(1)}) custom-call(s32[22]{0:T(128)S(1)} %get-tuple-element.19.meta, f32[4,8,512]{2,1,0:T(8,128)S(1)} %get-tuple-element.20.own), custom_call_target="tpu_custom_call" | custom-call | tf_op jit(solution)/shard_map/density_local/pallas_call | solution.py:613
  18.1 0.0 collective-permute-done.rec_odd
  18.1 0.0 all-to-all-done.rec
  18.1 6.0 %density_remote.1 = (f32[4,512]{1,0:T(4,128)}, f32[4,1,512]{2,1,0:T(1,128)S(1)}, f32[32,1,512]{2,1,0:T(1,128)}, s32[10]{0:T(128)S(1)}) custom-call(s32[22]{0:T(128)S(1)} %get-tuple-element.19.meta, f32[4,8,512]{2,1,0:T(8,128)S(1)} %get-tuple-element.20.own, f32[16,8,512]{2,1,0:T(8,128)S(1)} %all-to-all-done.rec, ...), custom_call_target="tpu_custom_call" | custom-call | tf_op jit(solution)/shard_map/density_remote/pallas_call | solution.py:623
  24.1 3.7 %all-to-all-start.1 = ((f32[32,1,512]{2,1,0:T(1,128)}), f32[32,1,512]{2,1,0:T(1,128)S(1)}, u32[]{:S(2)}, u32[]{:S(2)}) async-start(f32[32,1,512]{2,1,0:T(1,128)} %get-tuple-element.28), calls=%async_computation.1 | async-start | bytes 131072 | tf_op jit(solution)/shard_map/all_to_all | solution.py:646
  27.8 9.0 %force_local.1 = (f32[4,16,512]{2,1,0:T(8,128)S(1)}, f32[4,512,128]{2,1,0:T(8,128)S(1)}, f32[4,512,128]{2,1,0:T(8,128)S(1)}) custom-call(s32[22]{0:T(128)S(1)} %get-tuple-element.19.meta, f32[4,8,512]{2,1,0:T(8,128)S(1)} %get-tuple-element.20.own, f32[4,1,512]{2,1,0:T(1,128)S(1)} %get-tuple-element.27.term, bf16[4,512,64]{2,1,0:T(8,128)(2,1)S(1)} %get-tuple-element.29.left), custom_call_target="tpu_custom_call" | custom-call | tf_op jit(solution)/shard_map/force_local/pallas_call | solution.py:648
  36.8 0.0 all-to-all-done.1.rterm
  36.8 8.3 %force_remote.1 = (f32[3,4,512]{2,1,0:T(4,128)}, f32[4,512]{1,0:T(4,128)}) custom-call(s32[22]{0:T(128)S(1)} %get-tuple-element.19.meta, s32[10]{0:T(128)S(1)} %get-tuple-element.26.live, f32[4,8,512]{2,1,0:T(8,128)S(1)} %get-tuple-element.20.own, f32[16,8,512]{2,1,0:T(8,128)S(1)} %all-to-all-done.rec, f32[1,8,512]{2,1,0:T(8,128)S(1)} %collective-permute-done.rec_odd, ...), custom_call_target="tpu_custom_call" | custom-call | tf_op jit(solution)/shard_map/force_remote/pallas_call | solution.py:665
Async XLA Ops:
  2.3 15.8 %all-to-all-start = ((f32[16,8,512]{2,1,0:T(8,128)}), f32[16,8,512]{2,1,0:T(8,128)S(1)}, u32[]{:S(2)}, u32[]{:S(2)}) async-start(f32[16,8,512]{2,1,0:T(8,128)} %get-tuple-element.21), calls=%async_computation | async-start | bytes 524288 | tf_op jit(solution)/shard_map/all_to_all | solution.py:611
  7.9 10.2 %collective-permute-start = (f32[1,8,512]{2,1,0:T(8,128)S(1)}, f32[1,8,512]{2,1,0:T(8,128)S(1)}, u32[]{:S(2)}, u32[]{:S(2)}) collective-permute-start(f32[1,8,512]{2,1,0:T(8,128)S(1)} %get-tuple-element.22), channel_id=1, source_target_pairs={{8,16},{16,8},{9,17},{17,9},{10,18},{18,10},{11,19},{19,11},{12,20... | collective-permute-start | bytes 49160 | tf_op jit(solution)/shard_map/ppermute | solution.py:610
  24.1 12.7 %all-to-all-start.1 = ((f32[32,1,512]{2,1,0:T(1,128)}), f32[32,1,512]{2,1,0:T(1,128)S(1)}, u32[]{:S(2)}, u32[]{:S(2)}) async-start(f32[32,1,512]{2,1,0:T(1,128)} %get-tuple-element.28), calls=%async_computation.1 | async-start | bytes 131072 | tf_op jit(solution)/shard_map/all_to_all | solution.py:646

commit v2 on v1

--- a/solution.py
+++ b/solution.py
@@ -265,15 +265,14 @@
 
     def step(k, state):
         for g in range(group):
-            _, b, _, jstart, w = blocks.read(k * group + g)
-            weight = mrow[b, :, pl.ds(jstart, jcut)] * w
-            weight = jnp.concatenate([weight] * (STRIP // 8), axis=0)
+            _, b, _, jstart, _ = blocks.read(k * group + g)
+            root = jnp.concatenate([mrow[b, 0:8, pl.ds(jstart, jcut)]] * (STRIP // 8), axis=0)
+            half = jnp.concatenate([mrow[b, 8:16, pl.ds(jstart, jcut)]] * (STRIP // 8), axis=0)
             for row in range(0, icut, STRIP):
                 s = jnp.maximum(dist[g][row : row + STRIP, :], TINY)
-                q = s * lax.rsqrt(s)
-                e = 1.0 - q
+                e = root - s * lax.rsqrt(s)
                 u = jnp.maximum(e, 0.0)
-                t = jnp.minimum(0.5 - (s * 3.0) * e, u * u * u) * weight
+                t = jnp.minimum(half - (s * 3.0) * e, u * u * u)
                 part = t[:, :LANES]
                 for at in range(1, jcut // LANES):
                     part = part + t[:, at * LANES : (at + 1) * LANES]
@@ -282,16 +281,20 @@
             state = blocks.write((k + 2) * group + g, state)
             blocks.distances((k + 1) * group + g, left, right, dist[g])
         for g in range(group):
-            a, _, istart, _, _ = blocks.read(k * group + g)
-            acc[a, pl.ds(istart, icut), :] += parts[g][...]
+            a, _, istart, _, w = blocks.read(k * group + g)
+            acc[a, pl.ds(istart, icut), :] += parts[g][...] * w
         return state
 
     lax.fori_loop(0, chunks(total, group), step, state)
 
 
 def density_source(rows, right, mrow, at):
-    right[at] = right_parts(right_comps(rows))
-    mrow[at] = jnp.broadcast_to(rows[3:4], mrow.shape[1:])
+    m = rows[3:4]
+    root = jnp.where(m > 0.0, jnp.exp(jnp.log(jnp.maximum(m, 1e-30)) * (1.0 / 3.0)), 0.0)
+    right[at] = right_parts(right_comps(rows) * (root * root))
+    shape = (8, rows.shape[1])
+    half = 0.5 * (root * root * root)
+    mrow[at] = jnp.concatenate([jnp.broadcast_to(root, shape), jnp.broadcast_to(half, shape)], axis=0)
 
 
 def spread_left(parts, left, cell):
@@ -362,14 +365,16 @@
 
     copy.wait()
     lane = lax.broadcasted_iota(jnp.int32, (1, slots), 1)
-    ones = jnp.ones((8, LANES), BF16)
+    ones = jnp.ones((8, 2 * LANES), BF16)
     for k in range(cells):
-        one, two, three = split3(acc[k])
-        total_row = jnp.zeros((8, slots), F32)
-        for part in (three, two, one):
-            total_row = total_row + lax.dot_general(
-                ones, part.astype(BF16), (((1,), (1,)), ((), ())), preferred_element_type=F32
-            )
+        one = acc[k].astype(BF16)
+        two = (acc[k] - one.astype(F32)).astype(BF16)
+        total_row = lax.dot_general(
+            ones,
+            jnp.concatenate([one, two], axis=1),
+            (((1,), (1,)), ((), ())),
+            preferred_element_type=F32,
+        )
         inv = 1.0 / own[k, 4:5, :]
         rho = total_row[0:1] * (16.0 / math.pi) * (inv * inv * inv)
         occupied = jnp.where(lane < meta[k], 1.0, 0.0)
@@ -571,7 +576,8 @@
     others = peers + 2
     most = max(cells * (cells - 1) // 2 + 3 * cells, cells * cells, others) + 1
     icut, jcut, group = 128, slots // 2, 8
-    ring = Blocks.FIELDS * (most * (slots // icut) * (slots // jcut) + 6 * group)
+    dcut, dgroup = 64, 16
+    ring = Blocks.FIELDS * (most * (slots // dcut) * (slots // jcut) + 6 * dgroup)
     shape = jax.ShapeDtypeStruct
     params = pltpu.CompilerParams(vmem_limit_bytes=20 * 1024 * 1024)
     send = send.reshape(peers)
@@ -582,7 +588,7 @@
         lambda x: pltpu.with_memory_space_constraint(x, pltpu.HBM), (integers, floats, energy)
     )
     lists = [pltpu.SMEM((Tiles.FIELDS * most,), jnp.int32), pltpu.SMEM((ring,), jnp.int32)]
-    density_work = [pltpu.VMEM((icut, jcut), F32)] * group + [pltpu.VMEM((icut, LANES), F32)] * group
+    density_work = [pltpu.VMEM((dcut, jcut), F32)] * dgroup + [pltpu.VMEM((dcut, LANES), F32)] * dgroup
     force_work = [pltpu.VMEM((icut, jcut), F32)] * group + [pltpu.VMEM((icut, jcut), BF16)] * (2 * group)
     wide = shape((cells, slots, LANES), F32)
     left_shape = shape((cells, slots, COLS), BF16)
@@ -611,17 +617,17 @@
     rec = lax.all_to_all(pay, ("side", "cell"), split_axis=0, concat_axis=0, tiled=True)
 
     acc, left, force_left = pl.pallas_call(
-        functools.partial(density_local_kernel, icut, jcut, group, lay),
+        functools.partial(density_local_kernel, dcut, jcut, dgroup, lay),
         out_shape=[wide, left_shape, left_shape],
         in_specs=[SMEM, VMEM],
         out_specs=[VMEM] * 3,
-        scratch_shapes=lists + [weight_shape(cells), pltpu.VMEM((cells, 8, slots), F32)] + density_work,
+        scratch_shapes=lists + [weight_shape(cells), pltpu.VMEM((cells, 16, slots), F32)] + density_work,
         compiler_params=params,
         name="density_local",
     )(meta, own)
 
     density, term, pay, live = pl.pallas_call(
-        functools.partial(density_remote_kernel, icut, jcut, group, lay),
+        functools.partial(density_remote_kernel, dcut, jcut, dgroup, lay),
         out_shape=[
             shape((cells, slots), F32),
             shape((cells, 1, slots), F32),
@@ -633,7 +639,7 @@
         scratch_shapes=lists
         + [
             weight_shape(others),
-            pltpu.VMEM((others, 8, slots), F32),
+            pltpu.VMEM((others, 16, slots), F32),
             pltpu.VMEM((cells, slots, LANES), F32),
             pltpu.VMEM(energy.shape, F32),
             pltpu.SemaphoreType.DMA,

time: 44.8 us -> 46.3 us (1.033)
  the two profiles are of different devices: /device:TPU:19 before, /device:TPU:9 now
where the time goes in v2:
time: 46.3 us; the launch traced here: 45.9 us
  Pallas kernels  34.2 us (74%)
  starting transfers between devices  11 us (24%)
  between operations  0.7 us (2%)
    pallas_call x1, Pallas kernels, on_device(): pl.pallas_call(functools.partial(density_local_kernel, dcut, jcut, dgroup...  9.1 us
    pallas_call x1, Pallas kernels, on_device(): pl.pallas_call(functools.partial(force_remote_kernel, icut, jcut, group,...  8.29 us
    pallas_call x1, Pallas kernels, on_device(): pl.pallas_call(functools.partial(force_local_kernel, icut, jcut, group, l...  7.94 us
    pallas_call x1, Pallas kernels, on_device(): pl.pallas_call(functools.partial(density_remote_kernel, dcut, jcut, dgrou...  7.21 us
    all_to_all x1, starting transfers between devices, on_device(): lax.all_to_all(pay, ('side', 'cell'), split_axis=0, concat_axis=0, tiled=...  5.53 us
    ppermute x1, starting transfers between devices, on_device(): rec_odd = lax.ppermute(odd, ('pair', 'side'), swap)  3.13 us
    all_to_all x1, starting transfers between devices, on_device(): lax.all_to_all(pay, ('pair', 'side', 'cell'), split_axis=0, concat_axis=0...  2.32 us
    pallas_call x1, Pallas kernels, on_device(): pl.pallas_call(functools.partial(prep_kernel, lay), out_shape=[shape((cel...  1.65 us
  transfers between devices with their start and end apart: 3, of which 0 were waited for; matrix products, arithmetic and copies ran while one was open for 0% of the time, Pallas kernels for 37%

profile of v2, /device:TPU:9, one launch (start us, length us, event | category | flops | bytes accessed | tf_op | source)
XLA Modules:
  0.0 45.9 jit_solution(3875744572624350858)
XLA Ops:
  0.6 1.6 %prep.1 = (f32[4,8,512]{2,1,0:T(8,128)S(1)}, f32[16,8,512]{2,1,0:T(8,128)}, f32[1,8,512]{2,1,0:T(8,128)S(1)}, s32[22]{0:T(128)S(1)}) custom-call(s32[4]{0:T(128)} %counts_in.1, s32[8]{0:T(128)} %bitcast.3, s32[1,1,2,4]{3,2,1,0:T(2,128)} %bitcast.2, s32[1,1,2]{2,1,0:T(1,128)} %edge_in.1, f32[3,4,512]{2,1,0:T(4,128)} %pos_in.1, f32[3,4,512]{2,1,0:T(4,128)} %vel_in.1, ...), custom_call_target="tpu_custom_call" | custom-call | tf_op jit(solution)/shard_map/prep/pallas_call | solution.py:597
  2.3 5.5 %all-to-all-start = ((f32[16,8,512]{2,1,0:T(8,128)}), f32[16,8,512]{2,1,0:T(8,128)S(1)}, u32[]{:S(2)}, u32[]{:S(2)}) async-start(f32[16,8,512]{2,1,0:T(8,128)} %get-tuple-element.21), calls=%async_computation | async-start | bytes 524288 | tf_op jit(solution)/shard_map/all_to_all | solution.py:617
  7.8 3.1 %collective-permute-start = (f32[1,8,512]{2,1,0:T(8,128)S(1)}, f32[1,8,512]{2,1,0:T(8,128)S(1)}, u32[]{:S(2)}, u32[]{:S(2)}) collective-permute-start(f32[1,8,512]{2,1,0:T(8,128)S(1)} %get-tuple-element.22), channel_id=1, source_target_pairs={{8,16},{16,8},{9,17},{17,9},{10,18},{18,10},{11,19},{19,11},{12,20... | collective-permute-start | bytes 49160 | tf_op jit(solution)/shard_map/ppermute | solution.py:616
  11.0 9.1 %density_local.1 = (f32[4,512,128]{2,1,0:T(8,128)S(1)}, bf16[4,512,64]{2,1,0:T(8,128)(2,1)S(1)}, bf16[4,512,64]{2,1,0:T(8,128)(2,1)S(1)}) custom-call(s32[22]{0:T(128)S(1)} %get-tuple-element.19.meta, f32[4,8,512]{2,1,0:T(8,128)S(1)} %get-tuple-element.20.own), custom_call_target="tpu_custom_call" | custom-call | tf_op jit(solution)/shard_map/density_local/pallas_call | solution.py:619
  20.1 0.0 collective-permute-done.rec_odd
  20.1 0.0 all-to-all-done.rec
  20.1 7.2 %density_remote.1 = (f32[4,512]{1,0:T(4,128)}, f32[4,1,512]{2,1,0:T(1,128)S(1)}, f32[32,1,512]{2,1,0:T(1,128)}, s32[10]{0:T(128)S(1)}) custom-call(s32[22]{0:T(128)S(1)} %get-tuple-element.19.meta, f32[4,8,512]{2,1,0:T(8,128)S(1)} %get-tuple-element.20.own, f32[16,8,512]{2,1,0:T(8,128)S(1)} %all-to-all-done.rec, ...), custom_call_target="tpu_custom_call" | custom-call | tf_op jit(solution)/shard_map/density_remote/pallas_call | solution.py:629
  27.3 2.3 %all-to-all-start.1 = ((f32[32,1,512]{2,1,0:T(1,128)}), f32[32,1,512]{2,1,0:T(1,128)S(1)}, u32[]{:S(2)}, u32[]{:S(2)}) async-start(f32[32,1,512]{2,1,0:T(1,128)} %get-tuple-element.28), calls=%async_computation.1 | async-start | bytes 131072 | tf_op jit(solution)/shard_map/all_to_all | solution.py:652
  29.6 7.9 %force_local.1 = (f32[4,16,512]{2,1,0:T(8,128)S(1)}, f32[4,512,128]{2,1,0:T(8,128)S(1)}, f32[4,512,128]{2,1,0:T(8,128)S(1)}) custom-call(s32[22]{0:T(128)S(1)} %get-tuple-element.19.meta, f32[4,8,512]{2,1,0:T(8,128)S(1)} %get-tuple-element.20.own, f32[4,1,512]{2,1,0:T(1,128)S(1)} %get-tuple-element.27.term, bf16[4,512,64]{2,1,0:T(8,128)(2,1)S(1)} %get-tuple-element.29.left), custom_call_target="tpu_custom_call" | custom-call | tf_op jit(solution)/shard_map/force_local/pallas_call | solution.py:654
  37.6 0.0 all-to-all-done.1.rterm
  37.6 8.3 %force_remote.1 = (f32[3,4,512]{2,1,0:T(4,128)}, f32[4,512]{1,0:T(4,128)}) custom-call(s32[22]{0:T(128)S(1)} %get-tuple-element.19.meta, s32[10]{0:T(128)S(1)} %get-tuple-element.26.live, f32[4,8,512]{2,1,0:T(8,128)S(1)} %get-tuple-element.20.own, f32[16,8,512]{2,1,0:T(8,128)S(1)} %all-to-all-done.rec, f32[1,8,512]{2,1,0:T(8,128)S(1)} %collective-permute-done.rec_odd, ...), custom_call_target="tpu_custom_call" | custom-call | tf_op jit(solution)/shard_map/force_remote/pallas_call | solution.py:671
Async XLA Ops:
  2.3 17.8 %all-to-all-start = ((f32[16,8,512]{2,1,0:T(8,128)}), f32[16,8,512]{2,1,0:T(8,128)S(1)}, u32[]{:S(2)}, u32[]{:S(2)}) async-start(f32[16,8,512]{2,1,0:T(8,128)} %get-tuple-element.21), calls=%async_computation | async-start | bytes 524288 | tf_op jit(solution)/shard_map/all_to_all | solution.py:617
  7.8 12.2 %collective-permute-start = (f32[1,8,512]{2,1,0:T(8,128)S(1)}, f32[1,8,512]{2,1,0:T(8,128)S(1)}, u32[]{:S(2)}, u32[]{:S(2)}) collective-permute-start(f32[1,8,512]{2,1,0:T(8,128)S(1)} %get-tuple-element.22), channel_id=1, source_target_pairs={{8,16},{16,8},{9,17},{17,9},{10,18},{18,10},{11,19},{19,11},{12,20... | collective-permute-start | bytes 49160 | tf_op jit(solution)/shard_map/ppermute | solution.py:616
  27.3 10.3 %all-to-all-start.1 = ((f32[32,1,512]{2,1,0:T(1,128)}), f32[32,1,512]{2,1,0:T(1,128)S(1)}, u32[]{:S(2)}, u32[]{:S(2)}) async-start(f32[32,1,512]{2,1,0:T(1,128)} %get-tuple-element.28), calls=%async_computation.1 | async-start | bytes 131072 | tf_op jit(solution)/shard_map/all_to_all | solution.py:652

commit v3 on v2

--- a/solution.py
+++ b/solution.py
@@ -576,7 +576,7 @@
     others = peers + 2
     most = max(cells * (cells - 1) // 2 + 3 * cells, cells * cells, others) + 1
     icut, jcut, group = 128, slots // 2, 8
-    dcut, dgroup = 64, 16
+    dcut, dgroup = 128, 8
     ring = Blocks.FIELDS * (most * (slots // dcut) * (slots // jcut) + 6 * dgroup)
     shape = jax.ShapeDtypeStruct
     params = pltpu.CompilerParams(vmem_limit_bytes=20 * 1024 * 1024)

time: 46.3 us -> 46.9 us (1.013)
  the two profiles are of different devices: /device:TPU:9 before, /device:TPU:21 now
where the time goes in v3:
time: 46.9 us
  Pallas kernels  34.9 us (74%)
  starting transfers between devices  11.2 us (24%)
  between operations  0.7 us (1%)
    pallas_call x1, Pallas kernels, on_device(): pl.pallas_call(functools.partial(force_remote_kernel, icut, jcut, group,...  9.27 us
    pallas_call x1, Pallas kernels, on_device(): pl.pallas_call(functools.partial(force_local_kernel, icut, jcut, group, l...  8.96 us
    pallas_call x1, Pallas kernels, on_device(): pl.pallas_call(functools.partial(density_local_kernel, dcut, jcut, dgroup...  8.21 us
    pallas_call x1, Pallas kernels, on_device(): pl.pallas_call(functools.partial(density_remote_kernel, dcut, jcut, dgrou...  6.85 us
    all_to_all x1, starting transfers between devices, on_device(): lax.all_to_all(pay, ('side', 'cell'), split_axis=0, concat_axis=0, tiled=...  5.58 us
    all_to_all x1, starting transfers between devices, on_device(): lax.all_to_all(pay, ('pair', 'side', 'cell'), split_axis=0, concat_axis=0...  3.71 us
    ppermute x1, starting transfers between devices, on_device(): rec_odd = lax.ppermute(odd, ('pair', 'side'), swap)  1.96 us
    pallas_call x1, Pallas kernels, on_device(): pl.pallas_call(functools.partial(prep_kernel, lay), out_shape=[shape((cel...  1.65 us
  transfers between devices with their start and end apart: 3, of which 0 were waited for; matrix products, arithmetic and copies ran while one was open for 0% of the time, Pallas kernels for 37%

profile of v3, /device:TPU:21, one launch (start us, length us, event | category | flops | bytes accessed | tf_op | source)
XLA Modules:
  0.0 46.9 jit_solution(4275683382990675596)
XLA Ops:
  0.6 1.6 %prep.1 = (f32[4,8,512]{2,1,0:T(8,128)S(1)}, f32[16,8,512]{2,1,0:T(8,128)}, f32[1,8,512]{2,1,0:T(8,128)S(1)}, s32[22]{0:T(128)S(1)}) custom-call(s32[4]{0:T(128)} %counts_in.1, s32[8]{0:T(128)} %bitcast.3, s32[1,1,2,4]{3,2,1,0:T(2,128)} %bitcast.2, s32[1,1,2]{2,1,0:T(1,128)} %edge_in.1, f32[3,4,512]{2,1,0:T(4,128)} %pos_in.1, f32[3,4,512]{2,1,0:T(4,128)} %vel_in.1, ...), custom_call_target="tpu_custom_call" | custom-call | tf_op jit(solution)/shard_map/prep/pallas_call | solution.py:597
  2.3 5.6 %all-to-all-start = ((f32[16,8,512]{2,1,0:T(8,128)}), f32[16,8,512]{2,1,0:T(8,128)S(1)}, u32[]{:S(2)}, u32[]{:S(2)}) async-start(f32[16,8,512]{2,1,0:T(8,128)} %get-tuple-element.21), calls=%async_computation | async-start | bytes 524288 | tf_op jit(solution)/shard_map/all_to_all | solution.py:617
  7.9 2.0 %collective-permute-start = (f32[1,8,512]{2,1,0:T(8,128)S(1)}, f32[1,8,512]{2,1,0:T(8,128)S(1)}, u32[]{:S(2)}, u32[]{:S(2)}) collective-permute-start(f32[1,8,512]{2,1,0:T(8,128)S(1)} %get-tuple-element.22), channel_id=1, source_target_pairs={{8,16},{16,8},{9,17},{17,9},{10,18},{18,10},{11,19},{19,11},{12,20... | collective-permute-start | bytes 49160 | tf_op jit(solution)/shard_map/ppermute | solution.py:616
  9.8 8.2 %density_local.1 = (f32[4,512,128]{2,1,0:T(8,128)S(1)}, bf16[4,512,64]{2,1,0:T(8,128)(2,1)S(1)}, bf16[4,512,64]{2,1,0:T(8,128)(2,1)S(1)}) custom-call(s32[22]{0:T(128)S(1)} %get-tuple-element.19.meta, f32[4,8,512]{2,1,0:T(8,128)S(1)} %get-tuple-element.20.own), custom_call_target="tpu_custom_call" | custom-call | tf_op jit(solution)/shard_map/density_local/pallas_call | solution.py:619
  18.1 0.0 collective-permute-done.rec_odd
  18.1 0.0 all-to-all-done.rec
  18.1 6.9 %density_remote.1 = (f32[4,512]{1,0:T(4,128)}, f32[4,1,512]{2,1,0:T(1,128)S(1)}, f32[32,1,512]{2,1,0:T(1,128)}, s32[10]{0:T(128)S(1)}) custom-call(s32[22]{0:T(128)S(1)} %get-tuple-element.19.meta, f32[4,8,512]{2,1,0:T(8,128)S(1)} %get-tuple-element.20.own, f32[16,8,512]{2,1,0:T(8,128)S(1)} %all-to-all-done.rec, ...), custom_call_target="tpu_custom_call" | custom-call | tf_op jit(solution)/shard_map/density_remote/pallas_call | solution.py:629
  24.9 3.7 %all-to-all-start.1 = ((f32[32,1,512]{2,1,0:T(1,128)}), f32[32,1,512]{2,1,0:T(1,128)S(1)}, u32[]{:S(2)}, u32[]{:S(2)}) async-start(f32[32,1,512]{2,1,0:T(1,128)} %get-tuple-element.28), calls=%async_computation.1 | async-start | bytes 131072 | tf_op jit(solution)/shard_map/all_to_all | solution.py:652
  28.7 9.0 %force_local.1 = (f32[4,16,512]{2,1,0:T(8,128)S(1)}, f32[4,512,128]{2,1,0:T(8,128)S(1)}, f32[4,512,128]{2,1,0:T(8,128)S(1)}) custom-call(s32[22]{0:T(128)S(1)} %get-tuple-element.19.meta, f32[4,8,512]{2,1,0:T(8,128)S(1)} %get-tuple-element.20.own, f32[4,1,512]{2,1,0:T(1,128)S(1)} %get-tuple-element.27.term, bf16[4,512,64]{2,1,0:T(8,128)(2,1)S(1)} %get-tuple-element.29.left), custom_call_target="tpu_custom_call" | custom-call | tf_op jit(solution)/shard_map/force_local/pallas_call | solution.py:654
  37.6 0.0 all-to-all-done.1.rterm
  37.6 9.3 %force_remote.1 = (f32[3,4,512]{2,1,0:T(4,128)}, f32[4,512]{1,0:T(4,128)}) custom-call(s32[22]{0:T(128)S(1)} %get-tuple-element.19.meta, s32[10]{0:T(128)S(1)} %get-tuple-element.26.live, f32[4,8,512]{2,1,0:T(8,128)S(1)} %get-tuple-element.20.own, f32[16,8,512]{2,1,0:T(8,128)S(1)} %all-to-all-done.rec, f32[1,8,512]{2,1,0:T(8,128)S(1)} %collective-permute-done.rec_odd, ...), custom_call_target="tpu_custom_call" | custom-call | tf_op jit(solution)/shard_map/force_remote/pallas_call | solution.py:671
Async XLA Ops:
  2.3 15.8 %all-to-all-start = ((f32[16,8,512]{2,1,0:T(8,128)}), f32[16,8,512]{2,1,0:T(8,128)S(1)}, u32[]{:S(2)}, u32[]{:S(2)}) async-start(f32[16,8,512]{2,1,0:T(8,128)} %get-tuple-element.21), calls=%async_computation | async-start | bytes 524288 | tf_op jit(solution)/shard_map/all_to_all | solution.py:617
  7.9 10.2 %collective-permute-start = (f32[1,8,512]{2,1,0:T(8,128)S(1)}, f32[1,8,512]{2,1,0:T(8,128)S(1)}, u32[]{:S(2)}, u32[]{:S(2)}) collective-permute-start(f32[1,8,512]{2,1,0:T(8,128)S(1)} %get-tuple-element.22), channel_id=1, source_target_pairs={{8,16},{16,8},{9,17},{17,9},{10,18},{18,10},{11,19},{19,11},{12,20... | collective-permute-start | bytes 49160 | tf_op jit(solution)/shard_map/ppermute | solution.py:616
  24.9 12.7 %all-to-all-start.1 = ((f32[32,1,512]{2,1,0:T(1,128)}), f32[32,1,512]{2,1,0:T(1,128)S(1)}, u32[]{:S(2)}, u32[]{:S(2)}) async-start(f32[32,1,512]{2,1,0:T(1,128)} %get-tuple-element.28), calls=%async_computation.1 | async-start | bytes 131072 | tf_op jit(solution)/shard_map/all_to_all | solution.py:652
